TPU v7x, 256 devices: a whole 4x4x8 slice. The times are simulated.
256 devices in a mesh: polar: 32 (over z_hi, y, x), azimuth: 8 (over z_lo, core).
Axes of the slice: x: 4, y: 4, z: 8 (z_hi: 2, z_lo: 4; z = z_hi * 4 + z_lo), core: 2. Of those that a mesh axis runs over, the one named last changes fastest.
Arguments:
- features: bfloat16 [256, 1440, 256], P('polar', 'azimuth'), may hold values from -6 to 6
- cotangent: bfloat16 [256, 1440, 256], P('polar', 'azimuth'), may hold values from -6 to 6
- mixing: bfloat16 [256, 9, 256], replicated, may hold values from -0.125 to 0.125
- response: bfloat16 [9, 256, 9, 2, 720], P(None, 'polar', None, None, 'azimuth'), may hold values from -1.5 to 1.5
- offsets: int32 [256], P('polar'), may hold values from 0 to 247, as said below
Outputs:
- grad_features: bfloat16 [256, 1440, 256], P('polar', 'azimuth')
- grad_mixing: float32 [256, 9, 256], P('azimuth')
Inputs may be any that keep to these rules, and one draw needn't show every extreme that they name: offsets[l] lies from l - 8 up to l + 9 - 9 (that is l itself), clipped to 0 .. 247; in every aligned block of 8 rows one row takes each end of that range.
All inputs are finite; a program needn't handle non-finite values.
Results may differ from a plain program's by a relative error of at most 0.012.
Values may be sent and summed in bfloat16 or wider, within the bound.
No kernel may reach another device: no remote copies, remote signals or barrier semaphores. Data moves between devices by JAX's collectives and lax.ppermute only.
A program may use at most 128 MiB of HBM per device.

v0:
```python
import math

import jax
import jax.numpy as jnp
from jax import lax
from jax.experimental import pallas as pl
from jax.experimental.pallas import tpu as pltpu
from jax.sharding import Mesh
from jax.sharding import PartitionSpec as P

BF = jnp.bfloat16
F32 = jnp.float32

K = 9
BW = 9
C = 256
NLON = 1440
NM = 720
REACH = 8
GRP = 32
TM = 24
GM = 90
MB = 4

ROWS_AX = ("zh", "y")
MODE_AX = ("x", "zl", "co")
AZ_AX = ("zl", "co")


def mode_table():
    n = jnp.arange(NLON, dtype=jnp.int32)
    xq = jnp.arange(4, dtype=jnp.int32)
    g = jnp.arange(8, dtype=jnp.int32)
    first = (xq[:, None] * TM + g[None, :] * GM).reshape(32)
    t = jnp.arange(TM, dtype=jnp.int32)
    step = 2.0 * math.pi / NLON
    ang_a = (first[:, None] * n[None, :] % NLON).astype(F32) * step
    ang_b = (t[:, None] * n[None, :] % NLON).astype(F32) * step
    norm = 1.0 / math.sqrt(NLON)
    ca, sa = jnp.cos(ang_a) * norm, jnp.sin(ang_a) * norm
    cb, sb = jnp.cos(ang_b), jnp.sin(ang_b)
    ca, sa, cb, sb = lax.optimization_barrier((ca, sa, cb, sb))
    ca, sa = ca[:, None, :], sa[:, None, :]
    cb, sb = cb[None], sb[None]
    real = (xq[:, None, None] * TM + t[None, None, :] < GM) & (g[None, :, None] >= 0)
    real = real.reshape(32, TM)[:, :, None].astype(F32)
    table = jnp.stack(((ca * cb - sa * sb) * real, -(sa * cb + ca * sb) * real), axis=1)
    return table.astype(BF).reshape(32 * 2 * TM, NLON)


def shift(x, axis, by):
    length = lax.axis_size(axis)
    return lax.ppermute(x, axis, [(i, i + by) for i in range(length) if 0 <= i + by < length])


def ring_pieces(x, axis, dim=0):
    n = lax.axis_size(axis)
    me = lax.axis_index(axis)
    own = lax.dynamic_index_in_dim(x, me, dim, False)
    got = []
    for s in range(1, n):
        piece = lax.dynamic_index_in_dim(x, lax.rem(me + s, n), dim, False)
        got.append((s, lax.ppermute(piece, axis, [(i, (i + s) % n) for i in range(n)])))
    return own, got


def ring_exchange(x, axis):
    n = lax.axis_size(axis)
    me = lax.axis_index(axis)
    own, got = ring_pieces(x, axis)
    came = [piece for _, piece in got[::-1]] + [own]
    return lax.dynamic_slice_in_dim(jnp.stack(came + came[:-1]), n - 1 - me, n, 0)


def ring_sum(x, axis, dim=0):
    own, got = ring_pieces(x.astype(BF), axis, dim)
    total = own.astype(F32)
    for _, piece in got:
        total = total + piece.astype(F32)
    return total


def ring_gather(x, axis):
    n = lax.axis_size(axis)
    me = lax.axis_index(axis)
    came = []
    for s in range(n - 1, 0, -1):
        came.append(lax.ppermute(x, axis, [(i, (i + s) % n) for i in range(n)]))
    came.append(x)
    return lax.dynamic_slice_in_dim(jnp.stack(came + came[:-1]), n - 1 - me, n, 0)


def band_matrices(response, offsets):
    first = (lax.axis_index("zh") * 4 + lax.axis_index("y")) * GRP + lax.axis_index("x") * 8
    rel = (offsets - first - jnp.arange(8, dtype=jnp.int32)).astype(BF)
    flat = jnp.transpose(response, (4, 1, 0, 2, 3)).reshape(GM, 8, K * BW * 2)
    flat = jnp.pad(flat, ((0, 4 * TM - GM), (0, 0), (0, 0)))
    flat = jnp.concatenate((flat, jnp.broadcast_to(rel[None, :, None], (4 * TM, 8, 1))), axis=2)
    wide = K * BW * 2 + 1
    parts = ring_exchange(flat.reshape(4, TM, 8 * wide), "x")
    low = shift(parts[3], ROWS_AX, 1)
    high = shift(parts[0], ROWS_AX, -1)
    parts = parts.reshape(4, TM, 8, wide)
    own = jnp.transpose(parts, (1, 3, 0, 2)).reshape(TM, wide, GRP)
    halo = jnp.transpose(jnp.stack((low, high), 0).reshape(2, TM, 8, wide), (1, 3, 0, 2))
    halo = halo.reshape(TM, wide, 2 * REACH)

    def columns(v):
        resp = v[:, :-1].astype(F32).reshape(TM, K, BW, 2, v.shape[2])
        a, b = resp[:, :, :, 0], resp[:, :, :, 1]
        return jnp.stack((jnp.concatenate((a, b), -1), jnp.concatenate((-b, a), -1)), 3)

    value = jnp.concatenate((columns(own), columns(halo)), -1)
    place_own = own[0, -1].astype(jnp.int32) + jnp.arange(GRP, dtype=jnp.int32)
    rim = jnp.arange(REACH, dtype=jnp.int32)
    place_halo = halo[0, -1].astype(jnp.int32) + jnp.concatenate((rim - REACH, rim + GRP))
    place = jnp.concatenate((place_own, place_own, place_halo, place_halo))
    which = jnp.arange(GRP, dtype=jnp.int32)[:, None] - place[None, :]
    value = lax.optimization_barrier(value)
    dense = jnp.zeros((TM, K, 2, GRP, 96), F32)
    for j in range(BW):
        dense = jnp.where(which == j, value[:, :, j, :, None, :], dense)
    return dense.astype(BF).reshape(TM, K * 2 * GRP, 96)


def dual_kernel(band_ref, own_ref, halo_ref, mix_ref, z_ref, dual_ref, column_ref):
    for m in range(MB):
        column_ref[0:64, :] = own_ref[m]
        column_ref[64:96, :] = halo_ref[m]
        z = jnp.dot(band_ref[m], column_ref[...], preferred_element_type=F32).astype(BF)
        for k in range(K):
            z_ref[k, m] = z[k * 64 : (k + 1) * 64]
    total = jnp.zeros((MB * 64, C), F32)
    for k in range(K):
        total = total + jnp.dot(
            z_ref[k].reshape(MB * 64, C), mix_ref[k], preferred_element_type=F32
        )
    dual_ref[...] = total.astype(BF).reshape(MB, 64, C)


def dual_call(band, own, halo, mix):
    return pl.pallas_call(
        dual_kernel,
        grid=(TM // MB,),
        in_specs=[
            pl.BlockSpec((MB, K * 64, 96), lambda i: (i, 0, 0)),
            pl.BlockSpec((MB, 64, C), lambda i: (i, 0, 0)),
            pl.BlockSpec((MB, 32, C), lambda i: (i, 0, 0)),
            pl.BlockSpec((K, C, C), lambda i: (0, 0, 0)),
        ],
        out_specs=[
            pl.BlockSpec((K, MB, 64, C), lambda i: (0, i, 0, 0)),
            pl.BlockSpec((MB, 64, C), lambda i: (i, 0, 0)),
        ],
        out_shape=[
            jax.ShapeDtypeStruct((K, TM, 64, C), BF),
            jax.ShapeDtypeStruct((TM, 64, C), BF),
        ],
        scratch_shapes=[pltpu.VMEM((96, C), BF)],
        compiler_params=pltpu.CompilerParams(vmem_limit_bytes=40 * 1024 * 1024),
        cost_estimate=pl.CostEstimate(
            flops=2 * TM * 576 * C * 96 + 2 * TM * 64 * K * C * C,
            bytes_accessed=16_000_000,
            transcendentals=0,
        ),
    )(band, own, halo, mix)


def grad_kernel(spec_ref, z_ref, out_ref, turned_ref):
    @pl.when(pl.program_id(0) == 0)
    def _():
        turned_ref[...] = spec_ref[...].T

    product = jnp.dot(turned_ref[...], z_ref[0], preferred_element_type=F32)
    turned = product.T.astype(BF)
    for g in range(8):
        out_ref[g % 2, g // 2, 0] = turned[g * 32 : (g + 1) * 32]


def grad_call(spec, z):
    return pl.pallas_call(
        grad_kernel,
        grid=(K,),
        in_specs=[
            pl.BlockSpec((TM * 64, C), lambda k: (0, 0)),
            pl.BlockSpec((1, TM * 64, C), lambda k: (k, 0, 0)),
        ],
        out_specs=pl.BlockSpec((2, 4, 1, 32, C), lambda k: (0, 0, k, 0, 0)),
        out_shape=jax.ShapeDtypeStruct((2, 4, K, 32, C), BF),
        scratch_shapes=[pltpu.VMEM((C, TM * 64), BF)],
        compiler_params=pltpu.CompilerParams(vmem_limit_bytes=24 * 1024 * 1024),
        cost_estimate=pl.CostEstimate(
            flops=2 * TM * 64 * K * C * C, bytes_accessed=9_000_000, transcendentals=0
        ),
    )(spec, z)


def to_modes(spec):
    return lax.all_to_all(spec.reshape(32, 2 * TM, C), MODE_AX, 0, 0, tiled=True)


def by_mode(block):
    rows = block.shape[0]
    return jnp.transpose(block.reshape(rows, 2, TM, C), (2, 1, 0, 3))


def per_device(features, cotangent, mixing, response, offsets):
    cot_row = lax.all_to_all(cotangent, AZ_AX, 0, 0, tiled=True).reshape(NLON, C)
    table = mode_table()
    mix_basis = jnp.moveaxis(mixing, 1, 0)
    cot_row, response, offsets = lax.optimization_barrier((cot_row, response, offsets))
    band = band_matrices(response, offsets)
    feat_row = lax.all_to_all(features, AZ_AX, 0, 0, tiled=True).reshape(NLON, C)

    q = jnp.arange(32 * 2 * TM, dtype=jnp.int32)
    first_mode = (q // (2 * TM) == 0) & (q % TM == 0)
    weight = jnp.where(first_mode, 1.0, 2.0).astype(F32)[:, None]
    cospec = (jnp.dot(table, cot_row, preferred_element_type=F32) * weight).astype(BF)
    cospec = to_modes(cospec)
    low = shift(cospec[GRP - REACH :], ROWS_AX, 1)
    high = shift(cospec[:REACH], ROWS_AX, -1)
    own = by_mode(cospec).reshape(TM, 64, C)
    halo = by_mode(jnp.concatenate((low, high), 0)).reshape(TM, 32, C)

    spec = jnp.dot(table, feat_row, preferred_element_type=F32).astype(BF)
    spec = by_mode(to_modes(spec)).reshape(TM * 64, C)

    z, dual = dual_call(band, own, halo, mix_basis)

    dual = jnp.transpose(dual.reshape(TM, 2, GRP, C), (2, 1, 0, 3)).reshape(GRP, 2 * TM, C)
    dual_row = lax.all_to_all(dual, MODE_AX, 0, 0, tiled=True).reshape(32 * 2 * TM, C)
    grad = grad_call(spec, z.reshape(K, TM * 64, C)).reshape(2, 4, K * 32, C)
    grad = ring_sum(grad, "co").reshape(4, 4, 72, C)
    grad = ring_sum(grad, "x", 1).astype(BF)
    grad, dual_row = lax.optimization_barrier((grad, dual_row))
    cells = lax.dot_general(
        table, dual_row, (((0,), (0,)), ((), ())), preferred_element_type=F32
    ).astype(BF)
    cells = cells.reshape(8, NLON // 8, C)

    grad = jnp.transpose(grad.reshape(4, 4, 18, C), (1, 0, 2, 3)).reshape(16, 18, C)
    grad = lax.all_to_all(grad, ("y", "zl"), 0, 0, tiled=True)
    grad, cells = lax.optimization_barrier((grad, cells))
    grad = jnp.sum(grad.astype(F32), 0)
    grad = grad + lax.ppermute(grad, "zh", [(0, 1), (1, 0)])
    grad, cells = lax.optimization_barrier((grad, cells))
    grad_features = lax.all_to_all(cells, AZ_AX, 0, 0, tiled=True)
    grad = grad * (1.0 / math.sqrt(256 * NLON))
    grad = lax.all_gather(grad, ("y", "x"), axis=0, tiled=False).reshape(4, 4, 18, C)
    grad = jnp.transpose(grad, (1, 0, 2, 3))
    grad_mixing = jnp.transpose(grad.reshape(K, 32, C), (1, 0, 2))
    return grad_features, grad_mixing


def solution(mesh):
    fine = Mesh(mesh.devices.reshape(2, 4, 4, 4, 2), ("zh", "y", "x", "zl", "co"))
    rows = ("zh", "y", "x")
    return jax.shard_map(
        per_device,
        mesh=fine,
        in_specs=(
            P(rows, AZ_AX, None),
            P(rows, AZ_AX, None),
            P(),
            P(None, rows, None, None, AZ_AX),
            P(rows),
        ),
        out_specs=(P(rows, AZ_AX, None), P(AZ_AX, None, None)),
        check_vma=False,
    )
```

profile of v0, /device:TPU:32, one launch (start us, length us, event | category | flops | bytes accessed | tf_op | source)
XLA Modules:
  0.0 222.2 jit_solution(163832121508291247)
XLA Ops:
  0.6 2.2 copy.134
  2.8 6.0 %all-to-all-start.2 = ((bf16[8,180,256]{2,1,0:T(8,128)(2,1)}), bf16[8,180,256]{2,1,0:T(8,128)(2,1)S(1)}, u32[]{:S(2)}, u32[]{:S(2)}) async-start(bf16[8,180,256]{2,1,0:T(8,128)(2,1)} %copy.134), calls=%async_computation.2 | async-start | bytes 1507328 | tf_op jit(solution)/shard_map/all_to_all | solution.py:208
  8.9 1.3 fusion.25
  10.4 0.9 sine_multiply_fusion
  11.3 1.0 copy.132
  12.4 3.8 %subtract_multiply_fusion = (bf16[32,1,24,1440]{3,2,1,0:T(8,128)(2,1)S(1)}, bf16[32,1,24,1440]{3,2,1,0:T(8,128)(2,1)}) fusion(f32[32,24]{1,0:T(8,128)S(1)} %broadcast_bitcast_fusion, f32[24,1440]{1,0:T(8,128)} %get-tuple-element.20, f32[32,1440]{1,0:T(8,128)S(1)} %get-tuple-element.19, f32[24,1440]{1,0:T(8,128)} %get-tuple-element.18, ...), kind=kLoop, calls=%fused_computation.12 | loop fusion | flops 12165120 | bytes 5071872 | tf_op jit(solution)/shard_map/mul | solution.py:47
  16.2 9.5 %all-to-all-done.2 = bf16[8,180,256]{2,1,0:T(8,128)(2,1)S(1)} async-done(((bf16[8,180,256]{2,1,0:T(8,128)(2,1)}), bf16[8,180,256]{2,1,0:T(8,128)(2,1)S(1)}, u32[]{:S(2)}, u32[]{:S(2)}) %all-to-all-start.2) | async-done | bytes 737312 | tf_op jit(solution)/shard_map/all_to_all | solution.py:208
  25.7 7.6 %all-to-all-start = ((bf16[8,180,256]{2,1,0:T(8,128)(2,1)}), bf16[8,180,256]{2,1,0:T(8,128)(2,1)}, u32[]{:S(2)}, u32[]{:S(2)}) async-start(bf16[8,180,256]{2,1,0:T(8,128)(2,1)} %copy.132), calls=%async_computation | async-start | bytes 1507328 | tf_op jit(solution)/shard_map/all_to_all | solution.py:213
  33.2 4.3 %maximum_convert_fusion = bf16[32,2,24,1440]{3,2,1,0:T(8,128)(2,1)} fusion(bf16[32,1,24,1440]{3,2,1,0:T(8,128)(2,1)} %get-tuple-element.56, bf16[32,1,24,1440]{3,2,1,0:T(8,128)(2,1)S(1)} %get-tuple-element.55), kind=kLoop, calls=%fused_computation | loop fusion | flops 2211840 | bytes 8847360 | tf_op jit(solution)/shard_map/convert_element_type | solution.py:48
  37.9 0.4 copy.136
  38.3 0.4 reshape.275
  38.8 2.8 %collective-permute-start = (bf16[24,1304]{1,0:T(8,128)(2,1)S(1)}, bf16[24,1304]{1,0:T(8,128)(2,1)S(1)}, u32[]{:S(2)}, u32[]{:S(2)}) collective-permute-start(bf16[24,1304]{1,0:T(8,128)(2,1)S(1)} %get-tuple-element.68), channel_id=1, source_target_pairs={{0,24},{8,0},{16,8},{24,16},{1,25},{9,1},{17,9},{25,17},{2,26},{10... | collective-permute-start | bytes 187784 | tf_op jit(solution)/shard_map/ppermute | solution.py:63
  41.6 0.8 collective-permute-start.1
  42.4 0.9 collective-permute-start.2
  43.3 4.6 %fusion.9 = bf16[1536,256]{1,0:T(8,128)(2,1)} fusion(bf16[1536,1440]{1,0:T(8,128)(2,1)} %bitcast.189, bf16[1440,256]{1,0:T(8,128)(2,1)S(1)} %reshape.273, f32[1536]{0:T(1024)S(1)} %fusion.46), kind=kOutput, calls=%fused_computation.15 | convolution fusion | flops 1133248512 | bytes 5953536 | tf_op jit(solution)/shard_map/dot_general | solution.py:218
  47.9 2.1 all-to-all-done
  50.0 8.7 %all-to-all-start.3 = ((bf16[32,48,256]{2,1,0:T(8,128)(2,1)}), bf16[32,48,256]{2,1,0:T(8,128)(2,1)S(1)}, u32[]{:S(2)}, u32[]{:S(2)}) async-start(bf16[32,48,256]{2,1,0:T(8,128)(2,1)} %bitcast.57), calls=%async_computation.3 | async-start | bytes 1572864 | tf_op jit(solution)/shard_map/all_to_all | solution.py:199
  58.8 1.2 reshape.269
  60.0 4.6 %convolution_convert_fusion.1 = bf16[1536,256]{1,0:T(8,128)(2,1)} fusion(bf16[1536,1440]{1,0:T(8,128)(2,1)} %bitcast.190, bf16[1440,256]{1,0:T(8,128)(2,1)S(1)} %reshape.269), kind=kOutput, calls=%fused_computation.17 | convolution fusion | flops 1132855296 | bytes 5947392 | tf_op jit(solution)/shard_map/dot_general | solution.py:225
  64.8 0.6 reshape.276
  65.6 1.0 slice_convert_fusion
  66.6 3.5 %collective-permute-start.3 = (bf16[24,1304]{1,0:T(8,128)(2,1)S(1)}, bf16[24,1304]{1,0:T(8,128)(2,1)S(1)}, u32[]{:S(2)}, u32[]{:S(2)}) collective-permute-start(bf16[24,1304]{1,0:T(8,128)(2,1)S(1)} %get-tuple-element.62), channel_id=1, source_target_pairs={{0,32},{32,64},{64,96},{96,128},{128,160},{160,192},{192,224},{1,3... | collective-permute-start | bytes 187784 | tf_op jit(solution)/shard_map/ppermute | solution.py:53
  70.1 1.5 collective-permute-start.4
  71.6 2.1 copy.139
  74.0 1.5 maximum_bitcast_fusion.2
  75.6 0.7 collective-permute-done.4
  76.5 1.0 copy.140
  77.7 1.4 all-to-all-done.3
  79.1 6.5 %all-to-all-start.1 = ((bf16[32,48,256]{2,1,0:T(8,128)(2,1)}), bf16[32,48,256]{2,1,0:T(8,128)(2,1)}, u32[]{:S(2)}, u32[]{:S(2)}) async-start(bf16[32,48,256]{2,1,0:T(8,128)(2,1)} %bitcast.198), calls=%async_computation.1 | async-start | bytes 1572864 | tf_op jit(solution)/shard_map/all_to_all | solution.py:199
  86.2 0.7 copy.142
  86.9 1.7 pad_maximum_fusion.1
  90.0 0.8 fusion.52
  90.8 4.6 %collective-permute-start.5 = (bf16[8,48,256]{2,1,0:T(8,128)(2,1)}, bf16[8,48,256]{2,1,0:T(8,128)(2,1)}, u32[]{:S(2)}, u32[]{:S(2)}) collective-permute-start(bf16[8,48,256]{2,1,0:T(8,128)(2,1)} %get-tuple-element.53), channel_id=1, source_target_pairs={{0,32},{32,64},{64,96},{96,128},{128,160},{160,192},{192,224},{1,3... | collective-permute-start | bytes 589832 | tf_op jit(solution)/shard_map/ppermute | solution.py:53
  95.3 1.3 collective-permute-start.6
  96.9 4.5 %fusion.8.band_ref = bf16[24,576,96]{2,1,0:T(8,128)(2,1)S(1)} fusion(bf16[24,9,2,96]{3,2,1,0:T(2,128)(2,1)S(1)} %copy.160, bf16[24,9,2,96]{3,2,1,0:T(2,128)(2,1)S(1)} %copy.158, bf16[24,9,2,96]{3,2,1,0:T(2,128)(2,1)S(1)} %copy.156, bf16[24,9,2,96]{3,2,1,0:T(2,128)(2,1)S(1)} %copy.154, bf16[24,9,2,96]{3,2,1,0:T(2,128)(2,1)S(1)} %copy.152, ...), kind=kLoop, calls=%fused_computation.10 | loop fusion | flops 11943936 | bytes 3898368 | tf_op jit(solution)/shard_map/convert_element_type | solution.py:123
  101.4 1.1 copy.161
  102.5 3.5 %all-to-all-done.1 = bf16[32,48,256]{2,1,0:T(8,128)(2,1)} async-done(((bf16[32,48,256]{2,1,0:T(8,128)(2,1)}), bf16[32,48,256]{2,1,0:T(8,128)(2,1)}, u32[]{:S(2)}, u32[]{:S(2)}) %all-to-all-start.1) | async-done | bytes 786464 | tf_op jit(solution)/shard_map/all_to_all | solution.py:199
  106.0 2.3 %copy.133 = bf16[24,2,32,256]{3,2,1,0:T(8,128)(2,1)} copy(bf16[24,2,32,256]{3,0,1,2:T(8,128)(2,1)} %bitcast.4) | data formatting | bytes 1572864 | tf_op jit(solution)/shard_map/transpose | solution.py:204
  108.4 1.1 pad_maximum_fusion.2
  109.6 1.1 copy-done.3
  110.7 1.3 copy-done.4
  112.0 8.1 %shard_map.68 = (bf16[9,24,64,256]{3,2,1,0:T(8,128)(2,1)S(1)}, bf16[24,64,256]{2,1,0:T(8,128)(2,1)S(1)}) custom-call(bf16[24,576,96]{2,1,0:T(8,128)(2,1)S(1)} %fusion.8.band_ref, bf16[24,64,256]{2,1,0:T(8,128)(2,1)S(1)} %bitcast.180, bf16[24,32,256]{2,1,0:T(8,128)(2,1)S(1)} %bitcast.182, bf16[9,256,256]{2,1,0:T(8,128)(2,1)S(1)} %bitcast.183), custom_call_target="tpu_custom_call" | custom-call | flops 2491416576 | bytes 16000000 | tf_op jit(solution)/shard_map/pallas_call | solution.py:142
  120.0 2.9 %copy-done = bf16[9,24,64,256]{3,2,1,0:T(8,128)(2,1)} copy-done((bf16[9,24,64,256]{3,2,1,0:T(8,128)(2,1)}, bf16[9,24,64,256]{3,2,1,0:T(8,128)(2,1)S(1)}, u32[]{:S(2)}) %copy-start) | copy-done | bytes 7077912
  122.9 1.3 copy.164
  124.2 5.8 %all-to-all-start.4 = ((bf16[32,48,256]{2,1,0:T(8,128)(2,1)}), bf16[32,48,256]{2,1,0:T(8,128)(2,1)S(1)}, u32[]{:S(2)}, u32[]{:S(2)}) async-start(bf16[32,48,256]{2,1,0:T(8,128)(2,1)} %bitcast.76), calls=%async_computation.4 | async-start | bytes 1572864 | tf_op jit(solution)/shard_map/all_to_all | solution.py:231
  130.1 3.0 %copy-done.1 = bf16[9,24,64,256]{3,2,1,0:T(8,128)(2,1)S(1)} copy-done((bf16[9,24,64,256]{3,2,1,0:T(8,128)(2,1)S(1)}, bf16[9,24,64,256]{3,2,1,0:T(8,128)(2,1)}, u32[]{:S(2)}) %copy-start.1) | copy-done | bytes 7077912
  133.1 4.4 %shard_map.69 = bf16[2,4,9,32,256]{4,3,2,1,0:T(8,128)(2,1)S(1)} custom-call(bf16[1536,256]{1,0:T(8,128)(2,1)S(1)} %bitcast.179, bf16[9,1536,256]{2,1,0:T(8,128)(2,1)S(1)} %bitcast.176), custom_call_target="tpu_custom_call" | custom-call | flops 1811939328 | bytes 9000000 | tf_op jit(solution)/shard_map/pallas_call | solution.py:181
  137.6 0.5 collective-permute-start.7
  138.1 1.9 collective-permute-done.7
  140.1 0.5 copy.163
  140.7 2.9 %collective-permute-start.10 = (bf16[4,72,256]{2,0,1:T(4,128)(2,1)S(1)}, bf16[4,72,256]{2,0,1:T(4,128)(2,1)S(1)}, u32[]{:S(2)}, u32[]{:S(2)}) collective-permute-start(bf16[4,72,256]{2,0,1:T(4,128)(2,1)S(1)} %get-tuple-element.58), channel_id=1, source_target_pairs={{0,24},{8,0},{16,8},{24,16},{1,25},{9,1},{17,9},{25,17},{2,26},{10... | collective-permute-start | bytes 442376 | tf_op jit(solution)/shard_map/ppermute | solution.py:63
  143.6 2.3 %collective-permute-start.9 = (bf16[4,72,256]{2,0,1:T(4,128)(2,1)S(1)}, bf16[4,72,256]{2,0,1:T(4,128)(2,1)S(1)}, u32[]{:S(2)}, u32[]{:S(2)}) collective-permute-start(bf16[4,72,256]{2,0,1:T(4,128)(2,1)S(1)} %get-tuple-element.59), channel_id=1, source_target_pairs={{0,16},{8,24},{16,0},{24,8},{1,17},{9,25},{17,1},{25,9},{2,18},{10... | collective-permute-start | bytes 442376 | tf_op jit(solution)/shard_map/ppermute | solution.py:63
  145.9 5.9 %collective-permute-done.10 = bf16[4,72,256]{2,0,1:T(4,128)(2,1)S(1)} collective-permute-done((bf16[4,72,256]{2,0,1:T(4,128)(2,1)S(1)}, bf16[4,72,256]{2,0,1:T(4,128)(2,1)S(1)}, u32[]{:S(2)}, u32[]{:S(2)}) %collective-permute-start.10) | collective-permute-done | bytes 147488 | tf_op jit(solution)/shard_map/ppermute | solution.py:63
  151.8 3.0 %collective-permute-done.8 = bf16[4,72,256]{2,0,1:T(4,128)(2,1)S(1)} collective-permute-done((bf16[4,72,256]{2,0,1:T(4,128)(2,1)S(1)}, bf16[4,72,256]{2,0,1:T(4,128)(2,1)S(1)}, u32[]{:S(2)}, u32[]{:S(2)}) %collective-permute-start.8) | collective-permute-done | bytes 147488 | tf_op jit(solution)/shard_map/ppermute | solution.py:63
  155.1 0.7 copy.188
  155.8 22.3 %all-to-all-start.5 = ((bf16[16,18,256]{2,1,0:T(8,128)(2,1)}), bf16[16,18,256]{2,1,0:T(8,128)(2,1)S(1)}, u32[]{:S(2)}, u32[]{:S(2)}) async-start(bf16[16,18,256]{2,1,0:T(8,128)(2,1)} %bitcast.80), calls=%async_computation.5 | async-start | bytes 393216 | tf_op jit(solution)/shard_map/all_to_all | solution.py:242
  178.1 3.8 %convolution_convert_fusion = bf16[1440,256]{1,0:T(8,128)(2,1)S(1)} fusion(bf16[1536,1440]{1,0:T(8,128)(2,1)} %bitcast.191, bf16[1536,256]{1,0:T(8,128)(2,1)S(1)} %bitcast.199), kind=kOutput, calls=%fused_computation.16 | convolution fusion | flops 1132830720 | bytes 5947392 | tf_op jit(solution)/shard_map/dot_general | solution.py:236
  181.8 1.0 reshape.295
  182.8 3.0 %all-to-all-done.5 = bf16[16,18,256]{2,1,0:T(8,128)(2,1)S(1)} async-done(((bf16[16,18,256]{2,1,0:T(8,128)(2,1)}), bf16[16,18,256]{2,1,0:T(8,128)(2,1)S(1)}, u32[]{:S(2)}, u32[]{:S(2)}) %all-to-all-start.5) | async-done | bytes 147488 | tf_op jit(solution)/shard_map/all_to_all | solution.py:242
  186.3 7.7 %collective-permute-done.11 = f32[18,256]{1,0:T(8,128)S(1)} collective-permute-done((f32[18,256]{1,0:T(8,128)S(1)}, f32[18,256]{1,0:T(8,128)S(1)}, u32[]{:S(2)}, u32[]{:S(2)}) %collective-permute-start.11) | collective-permute-done | bytes 18464 | tf_op jit(solution)/shard_map/ppermute | solution.py:245
  194.0 4.2 %all-to-all-start.6 = ((bf16[8,180,256]{2,1,0:T(8,128)(2,1)}), bf16[8,180,256]{2,1,0:T(8,128)(2,1)S(1)}, u32[]{:S(2)}, u32[]{:S(2)}) async-start(bf16[8,180,256]{2,1,0:T(8,128)(2,1)} %reshape.295), calls=%async_computation.6 | async-start | bytes 1507328 | tf_op jit(solution)/shard_map/all_to_all | solution.py:247
  198.2 21.9 %all-gather.1 = f32[16,18,256]{2,1,0:T(8,128)S(1)} all-gather(f32[1,18,256]{2,1,0:T(8,128)S(1)} %multiply_bitcast_fusion), channel_id=2, replica_groups=mesh['zh'=2,'y'=4,'x'=4,'zl'=4,'co'=2] {'y','x'}, dimensions={0}, use_global_device_ids=true | all-gather | bytes 313344 | tf_op jit(solution)/shard_map/all_gather | solution.py:249
  220.4 0.8 reshape.297
  221.2 1.0 copy.169
  (96 shorter events, 5.3 us)
Async XLA Ops:
  0.6 10.6 %copy-start.7 = (bf16[8,180,256]{2,0,1:T(8,128)(2,1)S(1)}, bf16[8,180,256]{2,0,1:T(8,128)(2,1)}, u32[]{:S(2)}) copy-start(bf16[8,180,256]{2,0,1:T(8,128)(2,1)} %param.5) | copy-start | bytes 2211844
  2.8 22.8 %all-to-all-start.2 = ((bf16[8,180,256]{2,1,0:T(8,128)(2,1)}), bf16[8,180,256]{2,1,0:T(8,128)(2,1)S(1)}, u32[]{:S(2)}, u32[]{:S(2)}) async-start(bf16[8,180,256]{2,1,0:T(8,128)(2,1)} %copy.134), calls=%async_computation.2 | async-start | bytes 1507328 | tf_op jit(solution)/shard_map/all_to_all | solution.py:208
  25.7 24.4 %all-to-all-start = ((bf16[8,180,256]{2,1,0:T(8,128)(2,1)}), bf16[8,180,256]{2,1,0:T(8,128)(2,1)}, u32[]{:S(2)}, u32[]{:S(2)}) async-start(bf16[8,180,256]{2,1,0:T(8,128)(2,1)} %copy.132), calls=%async_computation | async-start | bytes 1507328 | tf_op jit(solution)/shard_map/all_to_all | solution.py:213
  33.2 4.4 %copy-start.8 = (bf16[9,8,9,2,90]{4,3,2,1,0:T(2,128)(2,1)S(1)}, bf16[9,8,9,2,90]{4,3,2,1,0:T(2,128)(2,1)}, u32[]{:S(2)}) copy-start(bf16[9,8,9,2,90]{4,3,2,1,0:T(2,128)(2,1)} %param.8) | copy-start | bytes 699844
  33.2 4.5 %copy-start.9 = (s32[8]{0:T(128)S(1)}, s32[8]{0:T(128)}, u32[]{:S(2)}) copy-start(s32[8]{0:T(128)} %param.9) | copy-start | bytes 100
  38.8 25.9 %collective-permute-start = (bf16[24,1304]{1,0:T(8,128)(2,1)S(1)}, bf16[24,1304]{1,0:T(8,128)(2,1)S(1)}, u32[]{:S(2)}, u32[]{:S(2)}) collective-permute-start(bf16[24,1304]{1,0:T(8,128)(2,1)S(1)} %get-tuple-element.68), channel_id=1, source_target_pairs={{0,24},{8,0},{16,8},{24,16},{1,25},{9,1},{17,9},{25,17},{2,26},{10... | collective-permute-start | bytes 187784 | tf_op jit(solution)/shard_map/ppermute | solution.py:63
  41.6 23.1 %collective-permute-start.1 = (bf16[24,1304]{1,0:T(8,128)(2,1)S(1)}, bf16[24,1304]{1,0:T(8,128)(2,1)S(1)}, u32[]{:S(2)}, u32[]{:S(2)}) collective-permute-start(bf16[24,1304]{1,0:T(8,128)(2,1)S(1)} %get-tuple-element.67), channel_id=1, source_target_pairs={{0,16},{8,24},{16,0},{24,8},{1,17},{9,25},{17,1},{25,9},{2,18},{10... | collective-permute-start | bytes 187784 | tf_op jit(solution)/shard_map/ppermute | solution.py:63
  42.4 22.3 %collective-permute-start.2 = (bf16[24,1304]{1,0:T(8,128)(2,1)S(1)}, bf16[24,1304]{1,0:T(8,128)(2,1)S(1)}, u32[]{:S(2)}, u32[]{:S(2)}) collective-permute-start(bf16[24,1304]{1,0:T(8,128)(2,1)S(1)} %get-tuple-element.66), channel_id=1, source_target_pairs={{0,8},{8,16},{16,24},{24,0},{1,9},{9,17},{17,25},{25,1},{2,10},{10... | collective-permute-start | bytes 187784 | tf_op jit(solution)/shard_map/ppermute | solution.py:63
  50.0 29.0 %all-to-all-start.3 = ((bf16[32,48,256]{2,1,0:T(8,128)(2,1)}), bf16[32,48,256]{2,1,0:T(8,128)(2,1)S(1)}, u32[]{:S(2)}, u32[]{:S(2)}) async-start(bf16[32,48,256]{2,1,0:T(8,128)(2,1)} %bitcast.57), calls=%async_computation.3 | async-start | bytes 1572864 | tf_op jit(solution)/shard_map/all_to_all | solution.py:199
  66.6 8.9 %collective-permute-start.3 = (bf16[24,1304]{1,0:T(8,128)(2,1)S(1)}, bf16[24,1304]{1,0:T(8,128)(2,1)S(1)}, u32[]{:S(2)}, u32[]{:S(2)}) collective-permute-start(bf16[24,1304]{1,0:T(8,128)(2,1)S(1)} %get-tuple-element.62), channel_id=1, source_target_pairs={{0,32},{32,64},{64,96},{96,128},{128,160},{160,192},{192,224},{1,3... | collective-permute-start | bytes 187784 | tf_op jit(solution)/shard_map/ppermute | solution.py:53
  70.1 6.2 %collective-permute-start.4 = (bf16[24,1304]{1,0:T(8,128)(2,1)S(1)}, bf16[24,1304]{1,0:T(8,128)(2,1)S(1)}, u32[]{:S(2)}, u32[]{:S(2)}) collective-permute-start(bf16[24,1304]{1,0:T(8,128)(2,1)S(1)} %get-tuple-element.63), channel_id=1, source_target_pairs={{32,0},{64,32},{96,64},{128,96},{160,128},{192,160},{224,192},{33,... | collective-permute-start | bytes 187784 | tf_op jit(solution)/shard_map/ppermute | solution.py:53
  79.1 10.9 %copy-start.5 = (bf16[32,48,256]{2,1,0:T(8,128)(2,1)}, bf16[32,48,256]{2,1,0:T(8,128)(2,1)S(1)}, u32[]{:S(2)}) copy-start(bf16[32,48,256]{2,1,0:T(8,128)(2,1)S(1)} %all-to-all-done.3) | copy-start | bytes 2359300
  79.1 27.0 %all-to-all-start.1 = ((bf16[32,48,256]{2,1,0:T(8,128)(2,1)}), bf16[32,48,256]{2,1,0:T(8,128)(2,1)}, u32[]{:S(2)}, u32[]{:S(2)}) async-start(bf16[32,48,256]{2,1,0:T(8,128)(2,1)} %bitcast.198), calls=%async_computation.1 | async-start | bytes 1572864 | tf_op jit(solution)/shard_map/all_to_all | solution.py:199
  90.8 10.6 %copy-start.6 = (bf16[32,48,256]{2,1,0:T(8,128)(2,1)S(1)}, bf16[32,48,256]{2,1,0:T(8,128)(2,1)}, u32[]{:S(2)}) copy-start(bf16[32,48,256]{2,1,0:T(8,128)(2,1)} %copy-done.5) | copy-start | bytes 2359300
  90.8 17.6 %collective-permute-start.5 = (bf16[8,48,256]{2,1,0:T(8,128)(2,1)}, bf16[8,48,256]{2,1,0:T(8,128)(2,1)}, u32[]{:S(2)}, u32[]{:S(2)}) collective-permute-start(bf16[8,48,256]{2,1,0:T(8,128)(2,1)} %get-tuple-element.53), channel_id=1, source_target_pairs={{0,32},{32,64},{64,96},{96,128},{128,160},{160,192},{192,224},{1,3... | collective-permute-start | bytes 589832 | tf_op jit(solution)/shard_map/ppermute | solution.py:53
  95.3 13.0 %collective-permute-start.6 = (bf16[8,48,256]{2,1,0:T(8,128)(2,1)}, bf16[8,48,256]{2,1,0:T(8,128)(2,1)}, u32[]{:S(2)}, u32[]{:S(2)}) collective-permute-start(bf16[8,48,256]{2,1,0:T(8,128)(2,1)} %get-tuple-element.54), channel_id=1, source_target_pairs={{32,0},{64,32},{96,64},{128,96},{160,128},{192,160},{224,192},{33,... | collective-permute-start | bytes 589832 | tf_op jit(solution)/shard_map/ppermute | solution.py:53
  109.5 1.1 copy-start.3
  110.7 1.3 copy-start.4
  120.0 2.9 %copy-start = (bf16[9,24,64,256]{3,2,1,0:T(8,128)(2,1)}, bf16[9,24,64,256]{3,2,1,0:T(8,128)(2,1)S(1)}, u32[]{:S(2)}) copy-start(bf16[9,24,64,256]{3,2,1,0:T(8,128)(2,1)S(1)} %get-tuple-element.24) | copy-start | bytes 21233668
  122.9 7.2 %copy-start.2 = (bf16[24,2,32,256]{3,2,1,0:T(8,128)(2,1)S(1)}, bf16[24,2,32,256]{3,2,1,0:T(8,128)(2,1)}, u32[]{:S(2)}) copy-start(bf16[24,2,32,256]{3,2,1,0:T(8,128)(2,1)} %copy.133) | copy-start | bytes 2359300
  124.2 30.8 %all-to-all-start.4 = ((bf16[32,48,256]{2,1,0:T(8,128)(2,1)}), bf16[32,48,256]{2,1,0:T(8,128)(2,1)S(1)}, u32[]{:S(2)}, u32[]{:S(2)}) async-start(bf16[32,48,256]{2,1,0:T(8,128)(2,1)} %bitcast.76), calls=%async_computation.4 | async-start | bytes 1572864 | tf_op jit(solution)/shard_map/all_to_all | solution.py:231
  130.1 3.0 %copy-start.1 = (bf16[9,24,64,256]{3,2,1,0:T(8,128)(2,1)S(1)}, bf16[9,24,64,256]{3,2,1,0:T(8,128)(2,1)}, u32[]{:S(2)}) copy-start(bf16[9,24,64,256]{3,2,1,0:T(8,128)(2,1)} %copy-done) | copy-start | bytes 21233668
  137.6 2.3 %collective-permute-start.7 = (bf16[4,288,256]{2,1,0:T(8,128)(2,1)S(1)}, bf16[4,288,256]{2,1,0:T(8,128)(2,1)S(1)}, u32[]{:S(2)}, u32[]{:S(2)}) collective-permute-start(bf16[4,288,256]{2,1,0:T(8,128)(2,1)S(1)} %dynamic-slice_bitcast_fusion), channel_id=1, source_target_pairs={{0,1},{1,0},{2,3},{3,2},{4,5},{5,4},{6,7},{7,6},{8,9},{9,8},{10,11... | collective-permute-start | bytes 1769480 | tf_op jit(solution)/shard_map/ppermute | solution.py:63
  140.7 11.1 %collective-permute-start.10 = (bf16[4,72,256]{2,0,1:T(4,128)(2,1)S(1)}, bf16[4,72,256]{2,0,1:T(4,128)(2,1)S(1)}, u32[]{:S(2)}, u32[]{:S(2)}) collective-permute-start(bf16[4,72,256]{2,0,1:T(4,128)(2,1)S(1)} %get-tuple-element.58), channel_id=1, source_target_pairs={{0,24},{8,0},{16,8},{24,16},{1,25},{9,1},{17,9},{25,17},{2,26},{10... | collective-permute-start | bytes 442376 | tf_op jit(solution)/shard_map/ppermute | solution.py:63
  143.6 11.2 %collective-permute-start.8 = (bf16[4,72,256]{2,0,1:T(4,128)(2,1)S(1)}, bf16[4,72,256]{2,0,1:T(4,128)(2,1)S(1)}, u32[]{:S(2)}, u32[]{:S(2)}) collective-permute-start(bf16[4,72,256]{2,0,1:T(4,128)(2,1)S(1)} %get-tuple-element.57), channel_id=1, source_target_pairs={{0,8},{8,16},{16,24},{24,0},{1,9},{9,17},{17,25},{25,1},{2,10},{10... | collective-permute-start | bytes 442376 | tf_op jit(solution)/shard_map/ppermute | solution.py:63
  143.6 11.2 %collective-permute-start.9 = (bf16[4,72,256]{2,0,1:T(4,128)(2,1)S(1)}, bf16[4,72,256]{2,0,1:T(4,128)(2,1)S(1)}, u32[]{:S(2)}, u32[]{:S(2)}) collective-permute-start(bf16[4,72,256]{2,0,1:T(4,128)(2,1)S(1)} %get-tuple-element.59), channel_id=1, source_target_pairs={{0,16},{8,24},{16,0},{24,8},{1,17},{9,25},{17,1},{25,9},{2,18},{10... | collective-permute-start | bytes 442376 | tf_op jit(solution)/shard_map/ppermute | solution.py:63
  155.8 30.1 %all-to-all-start.5 = ((bf16[16,18,256]{2,1,0:T(8,128)(2,1)}), bf16[16,18,256]{2,1,0:T(8,128)(2,1)S(1)}, u32[]{:S(2)}, u32[]{:S(2)}) async-start(bf16[16,18,256]{2,1,0:T(8,128)(2,1)} %bitcast.80), calls=%async_computation.5 | async-start | bytes 393216 | tf_op jit(solution)/shard_map/all_to_all | solution.py:242
  185.9 8.1 %collective-permute-start.11 = (f32[18,256]{1,0:T(8,128)S(1)}, f32[18,256]{1,0:T(8,128)S(1)}, u32[]{:S(2)}, u32[]{:S(2)}) collective-permute-start(f32[18,256]{1,0:T(8,128)S(1)} %convert_reduce_fusion), channel_id=1, source_target_pairs={{0,128},{128,0},{1,129},{129,1},{2,130},{130,2},{3,131},{131,3},{4... | collective-permute-start | bytes 55304 | tf_op jit(solution)/shard_map/ppermute | solution.py:245
  194.0 27.2 %all-to-all-start.6 = ((bf16[8,180,256]{2,1,0:T(8,128)(2,1)}), bf16[8,180,256]{2,1,0:T(8,128)(2,1)S(1)}, u32[]{:S(2)}, u32[]{:S(2)}) async-start(bf16[8,180,256]{2,1,0:T(8,128)(2,1)} %reshape.295), calls=%async_computation.6 | async-start | bytes 1507328 | tf_op jit(solution)/shard_map/all_to_all | solution.py:247
where the time goes:
time: 223 us; the launch traced here: 222 us
  starting transfers between devices  82.5 us (37%)
  waiting for transfers between devices  38.7 us (17%)
  local copies, waits for them, and re-layouts  30.3 us (14%)
  other arithmetic  22 us (10%)
  blocking collectives  21.9 us (10%)
  matrix products  13 us (6%)
  Pallas kernels  12.5 us (6%)
    all_to_all x1, starting transfers between devices, per_device(): grad = lax.all_to_all(grad, ('y', 'zl'), 0, 0, tiled=True)  22.3 us
    all_gather x1, blocking collectives, per_device(): lax.all_gather(grad, ('y', 'x'), axis=0, tiled=False).reshape(4, 4, 18, C)  21.9 us
    all_to_all x2, starting transfers between devices, to_modes(): lax.all_to_all(spec.reshape(32, 2 * TM, C), MODE_AX, 0, 0, tiled=True)  15.2 us
    unnamed x29, local copies, waits for them, and re-layouts  12.6 us
    ppermute x4, starting transfers between devices, shift(): lax.ppermute(x, axis, [(i, i + by) for i in range(length) if 0 <= i + by...  10.8 us
    ppermute x7, waiting for transfers between devices, ring_pieces(): lax.ppermute(piece, axis, [(i, (i + s) % n) for i in range(n)])  10.8 us
    ppermute x7, starting transfers between devices, ring_pieces(): lax.ppermute(piece, axis, [(i, (i + s) % n) for i in range(n)])  10.2 us
    all_to_all x1, waiting for transfers between devices, per_device(): lax.all_to_all(cotangent, AZ_AX, 0, 0, tiled=True).reshape(NLON, C)  9.45 us
  transfers between devices with their start and end apart: 19, of which 10 were waited for; matrix products, arithmetic and copies ran while one was open for 23% of the time, Pallas kernels for 2%

commit v1 on v0

--- a/solution.py
+++ b/solution.py
@@ -238,12 +238,11 @@
     ).astype(BF)
     cells = cells.reshape(8, NLON // 8, C)
 
-    grad = jnp.transpose(grad.reshape(4, 4, 18, C), (1, 0, 2, 3)).reshape(16, 18, C)
-    grad = lax.all_to_all(grad, ("y", "zl"), 0, 0, tiled=True)
+    grad = jnp.transpose(grad.reshape(4, 4, 18, C), (1, 0, 2, 3))[None]
+    grad = jnp.broadcast_to(grad, (2, 4, 4, 18, C)).reshape(32, 18, C)
+    grad = lax.all_to_all(grad, ("zh", "y", "zl"), 0, 0, tiled=True)
     grad, cells = lax.optimization_barrier((grad, cells))
     grad = jnp.sum(grad.astype(F32), 0)
-    grad = grad + lax.ppermute(grad, "zh", [(0, 1), (1, 0)])
-    grad, cells = lax.optimization_barrier((grad, cells))
     grad_features = lax.all_to_all(cells, AZ_AX, 0, 0, tiled=True)
     grad = grad * (1.0 / math.sqrt(256 * NLON))
     grad = lax.all_gather(grad, ("y", "x"), axis=0, tiled=False).reshape(4, 4, 18, C)

time: 223 us -> 222 us (level)
  waiting for transfers between devices: 38.7 us -> 36.1 us
    ppermute x1 -> x0, waiting for transfers between devices: 7.72 us -> none  [per_device(): grad = grad + lax.ppermute(grad, 'zh', [(0, 1), (1, 0)])]
    all_to_all x1, waiting for transfers between devices: 3.04 us -> 8.21 us  [per_device(): grad = lax.all_to_all(grad, ('zh', 'y', 'zl'), 0, 0, tiled=True)]
  transfers between devices with their start and end apart: 19 -> 18, of which waited for: 10 -> 9; matrix products, arithmetic and copies ran while one was open for 23% -> 23% of each run, Pallas kernels for 2% -> 2%
where the time goes in v1:
time: 222 us; the launch traced here: 221 us
  starting transfers between devices  83.4 us (38%)
  waiting for transfers between devices  36.1 us (16%)
  local copies, waits for them, and re-layouts  30.3 us (14%)
  other arithmetic  22.1 us (10%)
  blocking collectives  21.8 us (10%)
  matrix products  13 us (6%)
  Pallas kernels  12.5 us (6%)
    all_to_all x1, starting transfers between devices, per_device(): grad = lax.all_to_all(grad, ('zh', 'y', 'zl'), 0, 0, tiled=True)  22.5 us
    all_gather x1, blocking collectives, per_device(): lax.all_gather(grad, ('y', 'x'), axis=0, tiled=False).reshape(4, 4, 18, C)  21.8 us
    all_to_all x2, starting transfers between devices, to_modes(): lax.all_to_all(spec.reshape(32, 2 * TM, C), MODE_AX, 0, 0, tiled=True)  15.2 us
    unnamed x29, local copies, waits for them, and re-layouts  12.6 us
    ppermute x4, starting transfers between devices, shift(): lax.ppermute(x, axis, [(i, i + by) for i in range(length) if 0 <= i + by...  10.8 us
    ppermute x7, waiting for transfers between devices, ring_pieces(): lax.ppermute(piece, axis, [(i, (i + s) % n) for i in range(n)])  10.8 us
    ppermute x7, starting transfers between devices, ring_pieces(): lax.ppermute(piece, axis, [(i, (i + s) % n) for i in range(n)])  10.2 us
    all_to_all x1, waiting for transfers between devices, per_device(): lax.all_to_all(cotangent, AZ_AX, 0, 0, tiled=True).reshape(NLON, C)  9.46 us
  transfers between devices with their start and end apart: 18, of which 9 were waited for; matrix products, arithmetic and copies ran while one was open for 23% of the time, Pallas kernels for 2%

profile of v1, /device:TPU:32, one launch (start us, length us, event | category | flops | bytes accessed | tf_op | source)
XLA Modules:
  0.0 220.5 jit_solution(6872089221557208622)
XLA Ops:
  0.6 2.2 copy.211
  2.8 6.0 %all-to-all-start.2 = ((bf16[8,180,256]{2,1,0:T(8,128)(2,1)}), bf16[8,180,256]{2,1,0:T(8,128)(2,1)S(1)}, u32[]{:S(2)}, u32[]{:S(2)}) async-start(bf16[8,180,256]{2,1,0:T(8,128)(2,1)} %copy.211), calls=%async_computation.2 | async-start | bytes 1507328 | tf_op jit(solution)/shard_map/all_to_all | solution.py:208
  8.8 1.3 fusion.25
  10.3 0.9 sine_multiply_fusion
  11.3 1.0 copy.209
  12.4 3.8 %subtract_multiply_fusion = (bf16[32,1,24,1440]{3,2,1,0:T(8,128)(2,1)S(1)}, bf16[32,1,24,1440]{3,2,1,0:T(8,128)(2,1)}) fusion(f32[32,24]{1,0:T(8,128)S(1)} %broadcast_bitcast_fusion, f32[24,1440]{1,0:T(8,128)} %get-tuple-element.18, f32[32,1440]{1,0:T(8,128)S(1)} %get-tuple-element.17, f32[24,1440]{1,0:T(8,128)} %get-tuple-element.16, ...), kind=kLoop, calls=%fused_computation.12 | loop fusion | flops 12165120 | bytes 5071872 | tf_op jit(solution)/shard_map/mul | solution.py:47
  16.2 9.5 %all-to-all-done.2 = bf16[8,180,256]{2,1,0:T(8,128)(2,1)S(1)} async-done(((bf16[8,180,256]{2,1,0:T(8,128)(2,1)}), bf16[8,180,256]{2,1,0:T(8,128)(2,1)S(1)}, u32[]{:S(2)}, u32[]{:S(2)}) %all-to-all-start.2) | async-done | bytes 737312 | tf_op jit(solution)/shard_map/all_to_all | solution.py:208
  25.6 7.6 %all-to-all-start = ((bf16[8,180,256]{2,1,0:T(8,128)(2,1)}), bf16[8,180,256]{2,1,0:T(8,128)(2,1)}, u32[]{:S(2)}, u32[]{:S(2)}) async-start(bf16[8,180,256]{2,1,0:T(8,128)(2,1)} %copy.209), calls=%async_computation | async-start | bytes 1507328 | tf_op jit(solution)/shard_map/all_to_all | solution.py:213
  33.2 4.3 %maximum_convert_fusion = bf16[32,2,24,1440]{3,2,1,0:T(8,128)(2,1)} fusion(bf16[32,1,24,1440]{3,2,1,0:T(8,128)(2,1)} %get-tuple-element.56, bf16[32,1,24,1440]{3,2,1,0:T(8,128)(2,1)S(1)} %get-tuple-element.55), kind=kLoop, calls=%fused_computation | loop fusion | flops 2211840 | bytes 8847360 | tf_op jit(solution)/shard_map/convert_element_type | solution.py:48
  37.9 0.4 copy.213
  38.3 0.4 reshape.285
  38.7 2.8 %collective-permute-start = (bf16[24,1304]{1,0:T(8,128)(2,1)S(1)}, bf16[24,1304]{1,0:T(8,128)(2,1)S(1)}, u32[]{:S(2)}, u32[]{:S(2)}) collective-permute-start(bf16[24,1304]{1,0:T(8,128)(2,1)S(1)} %get-tuple-element.68), channel_id=1, source_target_pairs={{0,24},{8,0},{16,8},{24,16},{1,25},{9,1},{17,9},{25,17},{2,26},{10... | collective-permute-start | bytes 187784 | tf_op jit(solution)/shard_map/ppermute | solution.py:63
  41.6 0.8 collective-permute-start.1
  42.4 0.9 collective-permute-start.2
  43.3 4.6 %fusion.9 = bf16[1536,256]{1,0:T(8,128)(2,1)} fusion(bf16[1536,1440]{1,0:T(8,128)(2,1)} %bitcast.189, bf16[1440,256]{1,0:T(8,128)(2,1)S(1)} %reshape.283, f32[1536]{0:T(1024)S(1)} %fusion.46), kind=kOutput, calls=%fused_computation.15 | convolution fusion | flops 1133248512 | bytes 5953536 | tf_op jit(solution)/shard_map/dot_general | solution.py:218
  47.9 2.1 all-to-all-done
  50.0 8.7 %all-to-all-start.3 = ((bf16[32,48,256]{2,1,0:T(8,128)(2,1)}), bf16[32,48,256]{2,1,0:T(8,128)(2,1)S(1)}, u32[]{:S(2)}, u32[]{:S(2)}) async-start(bf16[32,48,256]{2,1,0:T(8,128)(2,1)} %bitcast.57), calls=%async_computation.3 | async-start | bytes 1572864 | tf_op jit(solution)/shard_map/all_to_all | solution.py:199
  58.7 1.2 reshape.279
  60.0 4.6 %convolution_convert_fusion.1 = bf16[1536,256]{1,0:T(8,128)(2,1)} fusion(bf16[1536,1440]{1,0:T(8,128)(2,1)} %bitcast.190, bf16[1440,256]{1,0:T(8,128)(2,1)S(1)} %reshape.279), kind=kOutput, calls=%fused_computation.17 | convolution fusion | flops 1132855296 | bytes 5947392 | tf_op jit(solution)/shard_map/dot_general | solution.py:225
  64.8 0.6 reshape.286
  65.6 1.0 slice_convert_fusion
  66.6 3.5 %collective-permute-start.3 = (bf16[24,1304]{1,0:T(8,128)(2,1)S(1)}, bf16[24,1304]{1,0:T(8,128)(2,1)S(1)}, u32[]{:S(2)}, u32[]{:S(2)}) collective-permute-start(bf16[24,1304]{1,0:T(8,128)(2,1)S(1)} %get-tuple-element.62), channel_id=1, source_target_pairs={{0,32},{32,64},{64,96},{96,128},{128,160},{160,192},{192,224},{1,3... | collective-permute-start | bytes 187784 | tf_op jit(solution)/shard_map/ppermute | solution.py:53
  70.1 1.5 collective-permute-start.4
  71.6 2.1 copy.216
  73.9 1.5 maximum_bitcast_fusion.2
  75.6 0.7 collective-permute-done.4
  76.5 1.0 copy.217
  77.7 1.4 all-to-all-done.3
  79.0 6.5 %all-to-all-start.1 = ((bf16[32,48,256]{2,1,0:T(8,128)(2,1)}), bf16[32,48,256]{2,1,0:T(8,128)(2,1)}, u32[]{:S(2)}, u32[]{:S(2)}) async-start(bf16[32,48,256]{2,1,0:T(8,128)(2,1)} %bitcast.198), calls=%async_computation.1 | async-start | bytes 1572864 | tf_op jit(solution)/shard_map/all_to_all | solution.py:199
  85.8 0.3 pad_maximum_fusion
  86.1 0.7 copy.219
  86.8 1.7 pad_maximum_fusion.1
  89.9 0.8 fusion.52
  90.7 4.6 %collective-permute-start.5 = (bf16[8,48,256]{2,1,0:T(8,128)(2,1)}, bf16[8,48,256]{2,1,0:T(8,128)(2,1)}, u32[]{:S(2)}, u32[]{:S(2)}) collective-permute-start(bf16[8,48,256]{2,1,0:T(8,128)(2,1)} %get-tuple-element.53), channel_id=1, source_target_pairs={{0,32},{32,64},{64,96},{96,128},{128,160},{160,192},{192,224},{1,3... | collective-permute-start | bytes 589832 | tf_op jit(solution)/shard_map/ppermute | solution.py:53
  95.3 1.3 collective-permute-start.6
  96.9 4.5 %fusion.8.band_ref = bf16[24,576,96]{2,1,0:T(8,128)(2,1)S(1)} fusion(bf16[24,9,2,96]{3,2,1,0:T(2,128)(2,1)S(1)} %copy.237, bf16[24,9,2,96]{3,2,1,0:T(2,128)(2,1)S(1)} %copy.235, bf16[24,9,2,96]{3,2,1,0:T(2,128)(2,1)S(1)} %copy.233, bf16[24,9,2,96]{3,2,1,0:T(2,128)(2,1)S(1)} %copy.231, bf16[24,9,2,96]{3,2,1,0:T(2,128)(2,1)S(1)} %copy.229, ...), kind=kLoop, calls=%fused_computation.10 | loop fusion | flops 11943936 | bytes 3898368 | tf_op jit(solution)/shard_map/convert_element_type | solution.py:123
  101.4 1.1 copy.238
  102.5 3.5 %all-to-all-done.1 = bf16[32,48,256]{2,1,0:T(8,128)(2,1)} async-done(((bf16[32,48,256]{2,1,0:T(8,128)(2,1)}), bf16[32,48,256]{2,1,0:T(8,128)(2,1)}, u32[]{:S(2)}, u32[]{:S(2)}) %all-to-all-start.1) | async-done | bytes 786464 | tf_op jit(solution)/shard_map/all_to_all | solution.py:199
  106.0 2.3 %copy.210 = bf16[24,2,32,256]{3,2,1,0:T(8,128)(2,1)} copy(bf16[24,2,32,256]{3,0,1,2:T(8,128)(2,1)} %bitcast.4) | data formatting | bytes 1572864 | tf_op jit(solution)/shard_map/transpose | solution.py:204
  108.3 1.1 pad_maximum_fusion.2
  109.5 1.1 copy-done.3
  110.6 1.3 copy-done.4
  111.9 8.1 %shard_map.68 = (bf16[9,24,64,256]{3,2,1,0:T(8,128)(2,1)S(1)}, bf16[24,64,256]{2,1,0:T(8,128)(2,1)S(1)}) custom-call(bf16[24,576,96]{2,1,0:T(8,128)(2,1)S(1)} %fusion.8.band_ref, bf16[24,64,256]{2,1,0:T(8,128)(2,1)S(1)} %bitcast.180, bf16[24,32,256]{2,1,0:T(8,128)(2,1)S(1)} %bitcast.182, bf16[9,256,256]{2,1,0:T(8,128)(2,1)S(1)} %bitcast.183), custom_call_target="tpu_custom_call" | custom-call | flops 2491416576 | bytes 16000000 | tf_op jit(solution)/shard_map/pallas_call | solution.py:142
  120.0 2.8 %copy-done = bf16[9,24,64,256]{3,2,1,0:T(8,128)(2,1)} copy-done((bf16[9,24,64,256]{3,2,1,0:T(8,128)(2,1)}, bf16[9,24,64,256]{3,2,1,0:T(8,128)(2,1)S(1)}, u32[]{:S(2)}) %copy-start) | copy-done | bytes 7077912
  122.8 1.3 copy.241
  124.2 5.8 %all-to-all-start.4 = ((bf16[32,48,256]{2,1,0:T(8,128)(2,1)}), bf16[32,48,256]{2,1,0:T(8,128)(2,1)S(1)}, u32[]{:S(2)}, u32[]{:S(2)}) async-start(bf16[32,48,256]{2,1,0:T(8,128)(2,1)} %bitcast.76), calls=%async_computation.4 | async-start | bytes 1572864 | tf_op jit(solution)/shard_map/all_to_all | solution.py:231
  130.1 3.0 %copy-done.1 = bf16[9,24,64,256]{3,2,1,0:T(8,128)(2,1)S(1)} copy-done((bf16[9,24,64,256]{3,2,1,0:T(8,128)(2,1)S(1)}, bf16[9,24,64,256]{3,2,1,0:T(8,128)(2,1)}, u32[]{:S(2)}) %copy-start.1) | copy-done | bytes 7077912
  133.1 4.4 %shard_map.69 = bf16[2,4,9,32,256]{4,3,2,1,0:T(8,128)(2,1)S(1)} custom-call(bf16[1536,256]{1,0:T(8,128)(2,1)S(1)} %bitcast.179, bf16[9,1536,256]{2,1,0:T(8,128)(2,1)S(1)} %bitcast.176), custom_call_target="tpu_custom_call" | custom-call | flops 1811939328 | bytes 9000000 | tf_op jit(solution)/shard_map/pallas_call | solution.py:181
  137.5 0.5 collective-permute-start.7
  138.0 1.9 collective-permute-done.7
  140.0 0.5 copy.240
  140.6 2.9 %collective-permute-start.10 = (bf16[4,72,256]{2,0,1:T(4,128)(2,1)S(1)}, bf16[4,72,256]{2,0,1:T(4,128)(2,1)S(1)}, u32[]{:S(2)}, u32[]{:S(2)}) collective-permute-start(bf16[4,72,256]{2,0,1:T(4,128)(2,1)S(1)} %get-tuple-element.58), channel_id=1, source_target_pairs={{0,24},{8,0},{16,8},{24,16},{1,25},{9,1},{17,9},{25,17},{2,26},{10... | collective-permute-start | bytes 442376 | tf_op jit(solution)/shard_map/ppermute | solution.py:63
  143.6 2.3 %collective-permute-start.9 = (bf16[4,72,256]{2,0,1:T(4,128)(2,1)S(1)}, bf16[4,72,256]{2,0,1:T(4,128)(2,1)S(1)}, u32[]{:S(2)}, u32[]{:S(2)}) collective-permute-start(bf16[4,72,256]{2,0,1:T(4,128)(2,1)S(1)} %get-tuple-element.59), channel_id=1, source_target_pairs={{0,16},{8,24},{16,0},{24,8},{1,17},{9,25},{17,1},{25,9},{2,18},{10... | collective-permute-start | bytes 442376 | tf_op jit(solution)/shard_map/ppermute | solution.py:63
  145.8 5.9 %collective-permute-done.10 = bf16[4,72,256]{2,0,1:T(4,128)(2,1)S(1)} collective-permute-done((bf16[4,72,256]{2,0,1:T(4,128)(2,1)S(1)}, bf16[4,72,256]{2,0,1:T(4,128)(2,1)S(1)}, u32[]{:S(2)}, u32[]{:S(2)}) %collective-permute-start.10) | collective-permute-done | bytes 147488 | tf_op jit(solution)/shard_map/ppermute | solution.py:63
  151.8 3.0 %collective-permute-done.8 = bf16[4,72,256]{2,0,1:T(4,128)(2,1)S(1)} collective-permute-done((bf16[4,72,256]{2,0,1:T(4,128)(2,1)S(1)}, bf16[4,72,256]{2,0,1:T(4,128)(2,1)S(1)}, u32[]{:S(2)}, u32[]{:S(2)}) %collective-permute-start.8) | collective-permute-done | bytes 147488 | tf_op jit(solution)/shard_map/ppermute | solution.py:63
  155.0 0.8 broadcast_in_dim.244
  155.8 22.5 %all-to-all-start.5 = ((bf16[32,18,256]{2,1,0:T(8,128)(2,1)}), bf16[32,18,256]{2,1,0:T(8,128)(2,1)S(1)}, u32[]{:S(2)}, u32[]{:S(2)}) async-start(bf16[32,18,256]{2,1,0:T(8,128)(2,1)} %bitcast.80), calls=%async_computation.5 | async-start | bytes 786432 | tf_op jit(solution)/shard_map/all_to_all | solution.py:243
  178.3 3.8 %convolution_convert_fusion = bf16[1440,256]{1,0:T(8,128)(2,1)S(1)} fusion(bf16[1536,1440]{1,0:T(8,128)(2,1)} %bitcast.191, bf16[1536,256]{1,0:T(8,128)(2,1)S(1)} %bitcast.199), kind=kOutput, calls=%fused_computation.16 | convolution fusion | flops 1132830720 | bytes 5947392 | tf_op jit(solution)/shard_map/dot_general | solution.py:236
  182.0 1.0 reshape.305
  183.0 8.2 %all-to-all-done.5 = bf16[32,18,256]{2,1,0:T(8,128)(2,1)S(1)} async-done(((bf16[32,18,256]{2,1,0:T(8,128)(2,1)}), bf16[32,18,256]{2,1,0:T(8,128)(2,1)S(1)}, u32[]{:S(2)}, u32[]{:S(2)}) %all-to-all-start.5) | async-done | bytes 294944 | tf_op jit(solution)/shard_map/all_to_all | solution.py:243
  191.2 5.3 %all-to-all-start.6 = ((bf16[8,180,256]{2,1,0:T(8,128)(2,1)}), bf16[8,180,256]{2,1,0:T(8,128)(2,1)S(1)}, u32[]{:S(2)}, u32[]{:S(2)}) async-start(bf16[8,180,256]{2,1,0:T(8,128)(2,1)} %reshape.305), calls=%async_computation.6 | async-start | bytes 1507328 | tf_op jit(solution)/shard_map/all_to_all | solution.py:246
  196.6 21.8 %all-gather.1 = f32[16,18,256]{2,1,0:T(8,128)S(1)} all-gather(f32[1,18,256]{2,1,0:T(8,128)S(1)} %multiply_bitcast_fusion), channel_id=2, replica_groups=mesh['zh'=2,'y'=4,'x'=4,'zl'=4,'co'=2] {'y','x'}, dimensions={0}, use_global_device_ids=true | all-gather | bytes 313344 | tf_op jit(solution)/shard_map/all_gather | solution.py:248
  218.8 0.8 reshape.307
  219.5 1.0 copy.246
  (94 shorter events, 4.6 us)
Async XLA Ops:
  0.6 10.6 %copy-start.7 = (bf16[8,180,256]{2,0,1:T(8,128)(2,1)S(1)}, bf16[8,180,256]{2,0,1:T(8,128)(2,1)}, u32[]{:S(2)}) copy-start(bf16[8,180,256]{2,0,1:T(8,128)(2,1)} %param.5) | copy-start | bytes 2211844
  2.8 22.8 %all-to-all-start.2 = ((bf16[8,180,256]{2,1,0:T(8,128)(2,1)}), bf16[8,180,256]{2,1,0:T(8,128)(2,1)S(1)}, u32[]{:S(2)}, u32[]{:S(2)}) async-start(bf16[8,180,256]{2,1,0:T(8,128)(2,1)} %copy.211), calls=%async_computation.2 | async-start | bytes 1507328 | tf_op jit(solution)/shard_map/all_to_all | solution.py:208
  25.6 24.4 %all-to-all-start = ((bf16[8,180,256]{2,1,0:T(8,128)(2,1)}), bf16[8,180,256]{2,1,0:T(8,128)(2,1)}, u32[]{:S(2)}, u32[]{:S(2)}) async-start(bf16[8,180,256]{2,1,0:T(8,128)(2,1)} %copy.209), calls=%async_computation | async-start | bytes 1507328 | tf_op jit(solution)/shard_map/all_to_all | solution.py:213
  33.2 4.4 %copy-start.8 = (bf16[9,8,9,2,90]{4,3,2,1,0:T(2,128)(2,1)S(1)}, bf16[9,8,9,2,90]{4,3,2,1,0:T(2,128)(2,1)}, u32[]{:S(2)}) copy-start(bf16[9,8,9,2,90]{4,3,2,1,0:T(2,128)(2,1)} %param.8) | copy-start | bytes 699844
  33.2 4.5 %copy-start.9 = (s32[8]{0:T(128)S(1)}, s32[8]{0:T(128)}, u32[]{:S(2)}) copy-start(s32[8]{0:T(128)} %param.9) | copy-start | bytes 100
  38.7 25.9 %collective-permute-start = (bf16[24,1304]{1,0:T(8,128)(2,1)S(1)}, bf16[24,1304]{1,0:T(8,128)(2,1)S(1)}, u32[]{:S(2)}, u32[]{:S(2)}) collective-permute-start(bf16[24,1304]{1,0:T(8,128)(2,1)S(1)} %get-tuple-element.68), channel_id=1, source_target_pairs={{0,24},{8,0},{16,8},{24,16},{1,25},{9,1},{17,9},{25,17},{2,26},{10... | collective-permute-start | bytes 187784 | tf_op jit(solution)/shard_map/ppermute | solution.py:63
  41.6 23.1 %collective-permute-start.1 = (bf16[24,1304]{1,0:T(8,128)(2,1)S(1)}, bf16[24,1304]{1,0:T(8,128)(2,1)S(1)}, u32[]{:S(2)}, u32[]{:S(2)}) collective-permute-start(bf16[24,1304]{1,0:T(8,128)(2,1)S(1)} %get-tuple-element.67), channel_id=1, source_target_pairs={{0,16},{8,24},{16,0},{24,8},{1,17},{9,25},{17,1},{25,9},{2,18},{10... | collective-permute-start | bytes 187784 | tf_op jit(solution)/shard_map/ppermute | solution.py:63
  42.4 22.3 %collective-permute-start.2 = (bf16[24,1304]{1,0:T(8,128)(2,1)S(1)}, bf16[24,1304]{1,0:T(8,128)(2,1)S(1)}, u32[]{:S(2)}, u32[]{:S(2)}) collective-permute-start(bf16[24,1304]{1,0:T(8,128)(2,1)S(1)} %get-tuple-element.66), channel_id=1, source_target_pairs={{0,8},{8,16},{16,24},{24,0},{1,9},{9,17},{17,25},{25,1},{2,10},{10... | collective-permute-start | bytes 187784 | tf_op jit(solution)/shard_map/ppermute | solution.py:63
  50.0 29.0 %all-to-all-start.3 = ((bf16[32,48,256]{2,1,0:T(8,128)(2,1)}), bf16[32,48,256]{2,1,0:T(8,128)(2,1)S(1)}, u32[]{:S(2)}, u32[]{:S(2)}) async-start(bf16[32,48,256]{2,1,0:T(8,128)(2,1)} %bitcast.57), calls=%async_computation.3 | async-start | bytes 1572864 | tf_op jit(solution)/shard_map/all_to_all | solution.py:199
  66.6 8.9 %collective-permute-start.3 = (bf16[24,1304]{1,0:T(8,128)(2,1)S(1)}, bf16[24,1304]{1,0:T(8,128)(2,1)S(1)}, u32[]{:S(2)}, u32[]{:S(2)}) collective-permute-start(bf16[24,1304]{1,0:T(8,128)(2,1)S(1)} %get-tuple-element.62), channel_id=1, source_target_pairs={{0,32},{32,64},{64,96},{96,128},{128,160},{160,192},{192,224},{1,3... | collective-permute-start | bytes 187784 | tf_op jit(solution)/shard_map/ppermute | solution.py:53
  70.1 6.2 %collective-permute-start.4 = (bf16[24,1304]{1,0:T(8,128)(2,1)S(1)}, bf16[24,1304]{1,0:T(8,128)(2,1)S(1)}, u32[]{:S(2)}, u32[]{:S(2)}) collective-permute-start(bf16[24,1304]{1,0:T(8,128)(2,1)S(1)} %get-tuple-element.63), channel_id=1, source_target_pairs={{32,0},{64,32},{96,64},{128,96},{160,128},{192,160},{224,192},{33,... | collective-permute-start | bytes 187784 | tf_op jit(solution)/shard_map/ppermute | solution.py:53
  79.0 10.9 %copy-start.5 = (bf16[32,48,256]{2,1,0:T(8,128)(2,1)}, bf16[32,48,256]{2,1,0:T(8,128)(2,1)S(1)}, u32[]{:S(2)}) copy-start(bf16[32,48,256]{2,1,0:T(8,128)(2,1)S(1)} %all-to-all-done.3) | copy-start | bytes 2359300
  79.0 27.0 %all-to-all-start.1 = ((bf16[32,48,256]{2,1,0:T(8,128)(2,1)}), bf16[32,48,256]{2,1,0:T(8,128)(2,1)}, u32[]{:S(2)}, u32[]{:S(2)}) async-start(bf16[32,48,256]{2,1,0:T(8,128)(2,1)} %bitcast.198), calls=%async_computation.1 | async-start | bytes 1572864 | tf_op jit(solution)/shard_map/all_to_all | solution.py:199
  90.7 10.6 %copy-start.6 = (bf16[32,48,256]{2,1,0:T(8,128)(2,1)S(1)}, bf16[32,48,256]{2,1,0:T(8,128)(2,1)}, u32[]{:S(2)}) copy-start(bf16[32,48,256]{2,1,0:T(8,128)(2,1)} %copy-done.5) | copy-start | bytes 2359300
  90.7 17.6 %collective-permute-start.5 = (bf16[8,48,256]{2,1,0:T(8,128)(2,1)}, bf16[8,48,256]{2,1,0:T(8,128)(2,1)}, u32[]{:S(2)}, u32[]{:S(2)}) collective-permute-start(bf16[8,48,256]{2,1,0:T(8,128)(2,1)} %get-tuple-element.53), channel_id=1, source_target_pairs={{0,32},{32,64},{64,96},{96,128},{128,160},{160,192},{192,224},{1,3... | collective-permute-start | bytes 589832 | tf_op jit(solution)/shard_map/ppermute | solution.py:53
  95.3 13.0 %collective-permute-start.6 = (bf16[8,48,256]{2,1,0:T(8,128)(2,1)}, bf16[8,48,256]{2,1,0:T(8,128)(2,1)}, u32[]{:S(2)}, u32[]{:S(2)}) collective-permute-start(bf16[8,48,256]{2,1,0:T(8,128)(2,1)} %get-tuple-element.54), channel_id=1, source_target_pairs={{32,0},{64,32},{96,64},{128,96},{160,128},{192,160},{224,192},{33,... | collective-permute-start | bytes 589832 | tf_op jit(solution)/shard_map/ppermute | solution.py:53
  109.5 1.1 copy-start.3
  110.6 1.3 copy-start.4
  120.0 2.9 %copy-start = (bf16[9,24,64,256]{3,2,1,0:T(8,128)(2,1)}, bf16[9,24,64,256]{3,2,1,0:T(8,128)(2,1)S(1)}, u32[]{:S(2)}) copy-start(bf16[9,24,64,256]{3,2,1,0:T(8,128)(2,1)S(1)} %get-tuple-element.22) | copy-start | bytes 21233668
  122.8 7.2 %copy-start.2 = (bf16[24,2,32,256]{3,2,1,0:T(8,128)(2,1)S(1)}, bf16[24,2,32,256]{3,2,1,0:T(8,128)(2,1)}, u32[]{:S(2)}) copy-start(bf16[24,2,32,256]{3,2,1,0:T(8,128)(2,1)} %copy.210) | copy-start | bytes 2359300
  124.2 30.8 %all-to-all-start.4 = ((bf16[32,48,256]{2,1,0:T(8,128)(2,1)}), bf16[32,48,256]{2,1,0:T(8,128)(2,1)S(1)}, u32[]{:S(2)}, u32[]{:S(2)}) async-start(bf16[32,48,256]{2,1,0:T(8,128)(2,1)} %bitcast.76), calls=%async_computation.4 | async-start | bytes 1572864 | tf_op jit(solution)/shard_map/all_to_all | solution.py:231
  130.0 3.0 %copy-start.1 = (bf16[9,24,64,256]{3,2,1,0:T(8,128)(2,1)S(1)}, bf16[9,24,64,256]{3,2,1,0:T(8,128)(2,1)}, u32[]{:S(2)}) copy-start(bf16[9,24,64,256]{3,2,1,0:T(8,128)(2,1)} %copy-done) | copy-start | bytes 21233668
  137.5 2.3 %collective-permute-start.7 = (bf16[4,288,256]{2,1,0:T(8,128)(2,1)S(1)}, bf16[4,288,256]{2,1,0:T(8,128)(2,1)S(1)}, u32[]{:S(2)}, u32[]{:S(2)}) collective-permute-start(bf16[4,288,256]{2,1,0:T(8,128)(2,1)S(1)} %dynamic-slice_bitcast_fusion), channel_id=1, source_target_pairs={{0,1},{1,0},{2,3},{3,2},{4,5},{5,4},{6,7},{7,6},{8,9},{9,8},{10,11... | collective-permute-start | bytes 1769480 | tf_op jit(solution)/shard_map/ppermute | solution.py:63
  140.6 11.1 %collective-permute-start.10 = (bf16[4,72,256]{2,0,1:T(4,128)(2,1)S(1)}, bf16[4,72,256]{2,0,1:T(4,128)(2,1)S(1)}, u32[]{:S(2)}, u32[]{:S(2)}) collective-permute-start(bf16[4,72,256]{2,0,1:T(4,128)(2,1)S(1)} %get-tuple-element.58), channel_id=1, source_target_pairs={{0,24},{8,0},{16,8},{24,16},{1,25},{9,1},{17,9},{25,17},{2,26},{10... | collective-permute-start | bytes 442376 | tf_op jit(solution)/shard_map/ppermute | solution.py:63
  143.6 11.2 %collective-permute-start.8 = (bf16[4,72,256]{2,0,1:T(4,128)(2,1)S(1)}, bf16[4,72,256]{2,0,1:T(4,128)(2,1)S(1)}, u32[]{:S(2)}, u32[]{:S(2)}) collective-permute-start(bf16[4,72,256]{2,0,1:T(4,128)(2,1)S(1)} %get-tuple-element.57), channel_id=1, source_target_pairs={{0,8},{8,16},{16,24},{24,0},{1,9},{9,17},{17,25},{25,1},{2,10},{10... | collective-permute-start | bytes 442376 | tf_op jit(solution)/shard_map/ppermute | solution.py:63
  143.6 11.2 %collective-permute-start.9 = (bf16[4,72,256]{2,0,1:T(4,128)(2,1)S(1)}, bf16[4,72,256]{2,0,1:T(4,128)(2,1)S(1)}, u32[]{:S(2)}, u32[]{:S(2)}) collective-permute-start(bf16[4,72,256]{2,0,1:T(4,128)(2,1)S(1)} %get-tuple-element.59), channel_id=1, source_target_pairs={{0,16},{8,24},{16,0},{24,8},{1,17},{9,25},{17,1},{25,9},{2,18},{10... | collective-permute-start | bytes 442376 | tf_op jit(solution)/shard_map/ppermute | solution.py:63
  155.8 35.4 %all-to-all-start.5 = ((bf16[32,18,256]{2,1,0:T(8,128)(2,1)}), bf16[32,18,256]{2,1,0:T(8,128)(2,1)S(1)}, u32[]{:S(2)}, u32[]{:S(2)}) async-start(bf16[32,18,256]{2,1,0:T(8,128)(2,1)} %bitcast.80), calls=%async_computation.5 | async-start | bytes 786432 | tf_op jit(solution)/shard_map/all_to_all | solution.py:243
  191.2 28.3 %all-to-all-start.6 = ((bf16[8,180,256]{2,1,0:T(8,128)(2,1)}), bf16[8,180,256]{2,1,0:T(8,128)(2,1)S(1)}, u32[]{:S(2)}, u32[]{:S(2)}) async-start(bf16[8,180,256]{2,1,0:T(8,128)(2,1)} %reshape.305), calls=%async_computation.6 | async-start | bytes 1507328 | tf_op jit(solution)/shard_map/all_to_all | solution.py:246
